TPU v7x, 32 devices: a whole 2x2x4 slice. The times are simulated.
32 devices in a mesh: aperture: 4 (over y, x), tile: 8 (over z, core).
Axes of the slice: x: 2, y: 2, z: 4, core: 2. Of those that a mesh axis runs over, the one named last changes fastest.
Arguments:
- sectors: bfloat16 [4, 96, 512, 2, 512], P('aperture', 'tile'), may hold values from -6 to 6
- footprint: int32 [4, 96, 2], P('aperture', 'tile'), may hold values from 0 to 6, as said below
- own_blocks: bfloat16 [6, 512, 512], replicated, may hold values from -0.25 to 0.25
- edge_blocks: bfloat16 [6, 128, 512], replicated, may hold values from -0.25 to 0.25
- edges: int32 [512, 2], P(('aperture', 'tile')), may hold values from 0 to 4096, as said below
Outputs:
- image: float32 [2, 512, 4096], P(None, ('aperture', 'tile'))
Inputs may be any that keep to these rules, and one draw needn't show every extreme that they name: `footprint`: per device, each group's 12 slots at one tile position hold first the live slots (own entry below 6), then dead ones with both entries 6; at least one slot is live; in every draw some device has all 12 slots live. The edge entry is 6 for every slot at the last tile position. `edges`: each interval spans at least 64 cells; in every draw some line starts at 0 and some line ends at 4096.
All inputs are finite; a program needn't handle non-finite values.
Results may differ from a plain program's by a relative error of at most 0.0003.
Values sent between devices are 32-bit elements; how exact they have to be, the bound alone decides.
A program may use at most 128 MiB of HBM per device.

v0:
```python
import math

import jax
import jax.numpy as jnp
from jax import lax
from jax.sharding import PartitionSpec as P

GORDER = 8


def from_behind(block, axis, distance):
    devices = range(lax.axis_size(axis))
    route = [(i - distance, i) for i in devices if i - distance in devices]
    return lax.ppermute(block, axis, route)


def gegen_fix(field, edges):
    width = field.shape[-1]
    cells = jnp.arange(width, dtype=jnp.int32)[None, :]
    lower = edges[:, 0:1]
    upper = edges[:, 1:2]
    span = (upper - lower).astype(jnp.float32)
    inside = (cells >= lower) & (cells < upper)
    offset = (cells - lower).astype(jnp.float32)
    xi_vals = jnp.where(inside, -1.0 + (2.0 * offset + 1.0) / span, 0.0)
    base = 1.0 - xi_vals * xi_vals
    weight = jnp.where(inside, base * jnp.sqrt(base), 0.0)
    prev = jnp.ones_like(xi_vals)
    curr = 4.0 * xi_vals
    rebuilt = jnp.zeros_like(field)
    for order in range(GORDER):
        poly = prev if order == 0 else curr
        numer = jnp.sum(weight * poly * field, axis=-1)
        denom = jnp.sum(weight * poly * poly, axis=-1)
        rebuilt = rebuilt + (numer / denom)[..., None] * poly
        if order >= 1:
            nxt = (2.0 * (order + 2) * xi_vals * curr - (order + 3) * prev) / (order + 1)
            prev, curr = (curr, nxt)
    return jnp.where(inside, rebuilt, field)


def phase_table(first, second, modulus):
    left = jnp.arange(first, dtype=jnp.int32)[:, None]
    right = jnp.arange(second, dtype=jnp.int32)[None, :]
    angle = 2.0 * math.pi / modulus * (left * right % modulus).astype(jnp.float32)
    return (jnp.cos(angle), jnp.sin(angle))


def spectral(field, tiles):
    lines = field.shape[1]
    width = field.shape[2]
    inner = width // tiles
    blocks = field.reshape(2, lines, tiles, inner)
    real_part, imag_part = (blocks[0], blocks[1])
    best = lax.Precision.HIGHEST
    cos_outer, sin_outer = phase_table(tiles, tiles, tiles)
    g_real = jnp.einsum("pt,ctm->cpm", cos_outer, real_part, precision=best) - jnp.einsum(
        "pt,ctm->cpm", sin_outer, imag_part, precision=best
    )
    g_imag = jnp.einsum("pt,ctm->cpm", sin_outer, real_part, precision=best) + jnp.einsum(
        "pt,ctm->cpm", cos_outer, imag_part, precision=best
    )
    cos_twist, sin_twist = phase_table(tiles, inner, width)
    h_real = g_real * cos_twist - g_imag * sin_twist
    h_imag = g_real * sin_twist + g_imag * cos_twist
    cos_inner, sin_inner = phase_table(inner, inner, inner)
    z_real = jnp.einsum("qm,cpm->cqp", cos_inner, h_real, precision=best) - jnp.einsum(
        "qm,cpm->cqp", sin_inner, h_imag, precision=best
    )
    z_imag = jnp.einsum("qm,cpm->cqp", sin_inner, h_real, precision=best) + jnp.einsum(
        "qm,cpm->cqp", cos_inner, h_imag, precision=best
    )
    scale = 1.0 / math.sqrt(width)
    return jnp.stack([z_real, z_imag]).reshape(2, lines, width) * scale


def on_device(sectors, footprint, own_blocks, edge_blocks, edges):
    data = sectors[0]
    foot = footprint[0]
    slots = data.shape[0]
    count_blocks = own_blocks.shape[0]
    tile_rows = own_blocks.shape[1]
    edge_rows = edge_blocks.shape[1]
    lines = data.shape[3]
    dims = (((0,), (1,)), ((), ()))

    def apply_kernel(block, kernel):
        return lax.dot_general(block, kernel, dims, preferred_element_type=jnp.float32)

    def visit(slot, carry):
        total, rim = carry
        block = lax.dynamic_index_in_dim(data, slot, 0, keepdims=False)
        own_index = foot[slot, 0]
        edge_index = foot[slot, 1]
        own_kernel = own_blocks[jnp.minimum(own_index, count_blocks - 1)]
        edge_kernel = edge_blocks[jnp.minimum(edge_index, count_blocks - 1)]
        total = total + jnp.where(own_index < count_blocks, apply_kernel(block, own_kernel), 0.0)
        rim = rim + jnp.where(edge_index < count_blocks, apply_kernel(block, edge_kernel), 0.0)
        return (total, rim)

    start = (
        jnp.zeros((2, lines, tile_rows), jnp.float32),
        jnp.zeros((2, lines, edge_rows), jnp.float32),
    )
    total, rim = lax.fori_loop(0, slots, visit, start)
    incoming = from_behind(rim, "tile", 1)
    total = jnp.concatenate([total[:, :, :edge_rows] + incoming, total[:, :, edge_rows:]], axis=2)
    groups = lax.axis_size("aperture")
    tiles = lax.axis_size("tile")
    per_device = lines // (groups * tiles)
    stacked = total.reshape(2, groups, tiles * per_device, tile_rows)
    summed = lax.psum_scatter(stacked, "aperture", scatter_dimension=1, tiled=True).reshape(
        2, tiles, per_device, tile_rows
    )
    gathered = lax.all_to_all(summed, "tile", split_axis=1, concat_axis=3, tiled=True)
    count = gathered.shape[2]
    field = spectral(gathered.reshape(2, count, -1), tiles).reshape(2, 1, count, -1)
    field = field.reshape(2, per_device, -1)
    return gegen_fix(field, edges)


def solution(mesh):
    in_specs = (
        P("aperture", "tile", None, None, None),
        P("aperture", "tile", None),
        P(),
        P(),
        P(("aperture", "tile"), None),
    )
    out_specs = P(None, ("aperture", "tile"), None)
    return jax.shard_map(
        on_device, mesh=mesh, in_specs=in_specs, out_specs=out_specs, check_vma=False
    )
```

profile of v0, /device:TPU:0, one launch (start us, length us, event | category | flops | bytes accessed | tf_op | source)
XLA Modules:
  0.0 271.0 jit_solution(1473990494419397077)
XLA Ops:
  6.5 30.9 %copy.17 = bf16[1,12,512,2,512]{2,4,3,1,0:T(8,128)(2,1)} copy(bf16[1,12,512,2,512]{4,3,2,1,0:T(2,128)(2,1)} %param.7) | data formatting | bytes 25165824 | tf_op args[0]
  37.5 89.4 %while.16 = (s32[]{:T(128)}, f32[2,512,512]{2,1,0:T(8,128)S(1)}, f32[2,512,128]{2,1,0:T(8,128)S(1)}, s32[12,2]{0,1:T(2,128)S(1)}, bf16[12,512,2,512]{1,3,2,0:T(8...) while((s32[]{:T(128)}, f32[2,512,512]{2,1,0:T(8,128)S(1)}, ...), condition=%wide.region_1.2_spmd.clone, body=%wide.region_0.1_spmd.clone.sunk | while | flops 673054720 | bytes 7997706 | solution.py:105
  39.5 2.4 select_add_fusion.2
  43.2 1.8 fusion.106
  44.9 0.7 constant_dynamic-slice_fusion.4
  47.0 2.4 select_add_fusion.2
  50.6 1.8 fusion.106
  52.4 0.7 constant_dynamic-slice_fusion.4
  54.4 2.4 select_add_fusion.2
  58.1 1.8 fusion.106
  59.8 0.7 constant_dynamic-slice_fusion.4
  61.9 2.4 select_add_fusion.2
  65.5 1.8 fusion.106
  67.3 0.7 constant_dynamic-slice_fusion.4
  69.3 2.4 select_add_fusion.2
  73.0 1.8 fusion.106
  74.7 0.7 constant_dynamic-slice_fusion.4
  76.8 2.4 select_add_fusion.2
  80.4 1.8 fusion.106
  84.2 2.4 select_add_fusion.2
  87.9 1.8 fusion.106
  91.7 2.4 select_add_fusion.2
  95.3 1.8 fusion.106
  99.1 2.4 select_add_fusion.2
  102.8 1.8 fusion.106
  106.6 2.4 select_add_fusion.2
  110.2 1.8 fusion.106
  114.0 2.4 select_add_fusion.2
  117.7 1.8 fusion.106
  121.5 2.4 select_add_fusion.2
  125.1 1.8 fusion.106
  126.9 2.4 collective-permute-start
  129.5 1.3 collective-permute-done
  130.9 1.6 pad_maximum_fusion
  133.8 2.4 broadcast_multiply_fusion.1
  136.2 75.5 %all-reduce.3.cloned.1.call-done = f32[2,4,128,512]{3,2,1,0:T(8,128)} async-done(((f32[2,4,128,512]{3,2,1,0:T(8,128)}), f32[2,4,128,512]{3,2,1,0:T(8,128)}) %all-reduce.3.cloned.1.call-update) | async-done | bytes 2097168
  211.6 1.7 constant_dynamic-slice_fusion.2
  213.4 0.8 copy.18
  214.2 4.6 %all-to-all-start = ((f32[2,8,16,512]{3,2,0,1:T(8,128)}), f32[2,8,16,512]{3,2,0,1:T(8,128)S(1)}, u32[]{:S(2)}, u32[]{:S(2)}) async-start(f32[2,8,16,512]{3,2,0,1:T(8,128)} %copy.18), calls=%async_computation | async-start | bytes 1048576 | tf_op jit(solution)/shard_map/all_to_all | solution.py:115
  219.0 15.1 %all-to-all-done = f32[2,8,16,512]{3,2,0,1:T(8,128)S(1)} async-done(((f32[2,8,16,512]{3,2,0,1:T(8,128)}), f32[2,8,16,512]{3,2,0,1:T(8,128)S(1)}, u32[]{:S(2)}, u32[]{:S(2)}) %all-to-all-start) | async-done | bytes 524320 | tf_op jit(solution)/shard_map/all_to_all | solution.py:115
  236.1 5.0 %fusion.22 = f32[16,8,512]{2,1,0:T(8,128)S(1)} fusion(f32[16,8,512]{2,1,0:T(8,128)S(1)} %fusion.11, f32[16,8,512]{2,1,0:T(8,128)S(1)} %fusion.12, f32[8,512]{1,0:T(8,128)S(1)} %fusion.46, f32[8,512]{1,0:T(8,128)S(1)} %fusion.47), kind=kOutput, calls=%fused_computation.34 | convolution fusion | flops 406519808 | bytes 819200 | tf_op jit(solution)/shard_map/qm,cpm->cqp/dot_general | solution.py:67
  241.1 5.7 %fusion.18 = f32[16,8,512]{2,1,0:T(8,128)} fusion(f32[16,8,512]{2,1,0:T(8,128)S(1)} %fusion.11, f32[16,8,512]{2,1,0:T(8,128)S(1)} %fusion.12, f32[8,512]{1,0:T(8,128)S(1)} %fusion.46, f32[8,512]{1,0:T(8,128)S(1)} %fusion.47), kind=kOutput, calls=%fused_computation.30 | convolution fusion | flops 406519808 | bytes 819200 | tf_op jit(solution)/shard_map/qm,cpm->cqp/dot_general | solution.py:70
  246.8 5.2 %fusion.14 = f32[16,512,8]{1,2,0:T(8,128)S(1)} fusion(f32[16,8,512]{2,1,0:T(8,128)S(1)} %fusion.22, f32[16,8,512]{2,1,0:T(8,128)S(1)} %fusion.11, f32[16,8,512]{2,1,0:T(8,128)S(1)} %fusion.12, f32[8,512]{1,0:T(8,128)S(1)} %fusion.46, f32[8,512]{1,0:T(8,128)S(1)} %fusion.47), kind=kOutput, calls=%fused_computation.26 | convolution fusion | flops 406585344 | bytes 1081344 | tf_op jit(solution)/shard_map/qm,cpm->cqp/dot_general | solution.py:67
  252.1 0.8 copy.20
  253.5 6.0 %fusion.13 = f32[16,512,8]{1,2,0:T(8,128)S(1)} fusion(f32[16,8,512]{2,1,0:T(8,128)} %fusion.18, f32[16,8,512]{2,1,0:T(8,128)} %copy-done.4, f32[16,8,512]{2,1,0:T(8,128)S(1)} %fusion.12, f32[8,512]{1,0:T(8,128)S(1)} %fusion.46, f32[8,512]{1,0:T(8,128)S(1)} %fusion.47), kind=kOutput, calls=%fused_computation.24 | convolution fusion | flops 406585344 | bytes 1081344 | tf_op jit(solution)/shard_map/qm,cpm->cqp/dot_general | solution.py:70
  259.5 0.8 copy.21
  260.9 2.0 multiply_reduce_fusion.7
  263.0 1.2 multiply_select_fusion
  (45 shorter events, 9.4 us)
Async XLA Ops:
  6.5 205.1 %all-reduce.3.cloned.1.call-start = ((), (), s32[]{:S(2)}) async-start(), calls=%async_computation.1 | async-start | bytes 4194304
  6.5 30.9 %copy-start.5 = (s32[1,12,2]{1,2,0:T(2,128)S(1)}, s32[1,12,2]{1,2,0:T(2,128)}, u32[]{:S(2)}) copy-start(s32[1,12,2]{1,2,0:T(2,128)} %param.8) | copy-start | bytes 292
  126.9 3.9 %collective-permute-start = (f32[2,512,128]{2,1,0:T(8,128)S(1)}, f32[2,512,128]{2,1,0:T(8,128)S(1)}, u32[]{:S(2)}, u32[]{:S(2)}) collective-permute-start(f32[2,512,128]{2,1,0:T(8,128)S(1)} %get-tuple-element.131), channel_id=1, source_target_pairs={{0,1},{1,2},{2,3},{3,4},{4,5},{5,6},{6,7},{8,9},{9,10},{10,11},{11... | collective-permute-start | bytes 1572872 | tf_op jit(solution)/shard_map/ppermute | solution.py:14
  132.5 0.7 copy-start.7
  132.5 1.3 copy-start.6
  214.2 20.0 %all-to-all-start = ((f32[2,8,16,512]{3,2,0,1:T(8,128)}), f32[2,8,16,512]{3,2,0,1:T(8,128)S(1)}, u32[]{:S(2)}, u32[]{:S(2)}) async-start(f32[2,8,16,512]{3,2,0,1:T(8,128)} %copy.18), calls=%async_computation | async-start | bytes 1048576 | tf_op jit(solution)/shard_map/all_to_all | solution.py:115
  236.1 10.7 %copy-start.4 = (f32[16,8,512]{2,1,0:T(8,128)}, f32[16,8,512]{2,1,0:T(8,128)S(1)}, u32[]{:S(2)}) copy-start(f32[16,8,512]{2,1,0:T(8,128)S(1)} %fusion.11) | copy-start | bytes 786436
  260.9 2.1 copy-start
  260.9 2.1 copy-start.1
  260.9 2.1 copy-start.2
  260.9 2.1 copy-start.3
Sparse Core Ops, SparseCore 0:
  132.6 78.9 all-reduce.2
where the time goes:
time: 273 us; the launch traced here: 271 us
  waiting for transfers between devices  92 us (34%)
  matrix products  73.7 us (27%)
  local copies, waits for them, and re-layouts  45.8 us (17%)
  loops' own time  31.4 us (12%)
  between operations  13.6 us (5%)
  other arithmetic  7.52 us (3%)
  starting transfers between devices  7 us (3%)
    unnamed x2, waiting for transfers between devices  75.5 us
    dot_general x24, matrix products, apply_kernel(): lax.dot_general(block, kernel, dims, preferred_element_type=jnp.float32)  50.2 us
    unnamed x19, local copies, waits for them, and re-layouts  33.9 us
    another operation x1, loops' own time, on_device(): total, rim = lax.fori_loop(0, slots, visit, start)  31.4 us
    all_to_all x1, waiting for transfers between devices, on_device(): lax.all_to_all(summed, 'tile', split_axis=1, concat_axis=3, tiled=True)  15.1 us
    dynamic_slice x12, local copies, waits for them, and re-layouts, visit(): edge_index = foot[slot, 1]  7.86 us
    dot_general x1, matrix products, spectral(): jnp.einsum('qm,cpm->cqp', cos_inner, h_imag, precision=best)  6.01 us
    dot_general x1, matrix products, spectral(): jnp.einsum('qm,cpm->cqp', sin_inner, h_real, precision=best)  5.72 us
  transfers between devices with their start and end apart: 3, of which 3 were waited for; matrix products, arithmetic and copies ran while one was open for 1% of the time, Pallas kernels for 0%

commit v1 on v0

--- a/solution.py
+++ b/solution.py
@@ -1,17 +1,295 @@
+import functools
 import math
 
 import jax
 import jax.numpy as jnp
+import ml_dtypes
+import numpy as np
 from jax import lax
+from jax.experimental import pallas as pl
+from jax.experimental.pallas import tpu as pltpu
 from jax.sharding import PartitionSpec as P
 
 GORDER = 8
-
-
-def from_behind(block, axis, distance):
-    devices = range(lax.axis_size(axis))
-    route = [(i - distance, i) for i in devices if i - distance in devices]
-    return lax.ppermute(block, axis, route)
+MESH = pl.DeviceIdType.MESH
+
+
+def partner(me, step, groups):
+    if groups == 4:
+        return [3 - me, me + 1 - 2 * lax.rem(me, 2), lax.rem(me + 2, 4)][step - 1]
+    return lax.rem(me + step, groups)
+
+
+def source(me, step, groups):
+    if groups == 4:
+        return partner(me, step, groups)
+    return lax.rem(me + groups - step, groups)
+
+
+def exchange_kernel(
+    groups, tiles, sec_ref, foot_ref, own_hbm, edge_hbm, out_ref,
+    held, own_ref, edge_ref, wide, part, arrived, snd, rcv,
+    load_sem, kern_sem, rs_send, rs_recv, tr_send, tr_recv,
+):
+    slots, samples = sec_ref.shape[0], sec_ref.shape[1]
+    blocks, cells = own_ref.shape[0], own_ref.shape[1]
+    rows, width = part.shape[1], part.shape[2] // 2
+    chunks = snd.shape[0]
+    piece = rows // chunks
+    per = snd.shape[3]
+    me = lax.axis_index("aperture")
+    tile = lax.axis_index("tile")
+    flat = sec_ref.reshape(slots, 2 * samples, sec_ref.shape[3])
+    order = [partner(me, step, groups) for step in range(1, groups)] + [me]
+
+    def load(step):
+        lanes = pl.ds(pl.multiple_of(order[step] * width, width), width)
+        return pltpu.make_async_copy(flat.at[:, :, lanes], held.at[step], load_sem.at[step])
+
+    kernels = [
+        pltpu.make_async_copy(own_hbm, own_ref, kern_sem.at[0]),
+        pltpu.make_async_copy(edge_hbm, edge_ref, kern_sem.at[1]),
+    ]
+    for copy in kernels:
+        copy.start()
+    for step in range(groups):
+        load(step).start()
+
+    barrier = pltpu.get_barrier_semaphore()
+    for step in range(1, groups):
+        pl.semaphore_signal(barrier, inc=1, device_id=(partner(me, step, groups), tile), device_id_type=MESH)
+    for step in range(1, tiles):
+        pl.semaphore_signal(barrier, inc=1, device_id=(me, lax.rem(tile + step, tiles)), device_id_type=MESH)
+    pl.semaphore_wait(barrier, groups + tiles - 2)
+    for copy in kernels:
+        copy.wait()
+
+    def reduce_copy(step, chunk):
+        span = pl.ds(chunk * piece, piece)
+        return pltpu.make_async_remote_copy(
+            src_ref=part.at[step - 1, span],
+            dst_ref=arrived.at[step - 1, span],
+            send_sem=rs_send.at[step - 1, chunk],
+            recv_sem=rs_recv.at[step - 1, chunk],
+            device_id=(partner(me, step, groups), tile),
+            device_id_type=MESH,
+        )
+
+    for step in range(groups):
+        load(step).wait()
+        part[step] = jnp.zeros((rows, 2 * width), jnp.float32)
+
+        @pl.loop(0, slots)
+        def _(slot):
+            wide[...] = held[step, slot].astype(jnp.float32)
+            data = jnp.concatenate(
+                [wide[pl.ds(0, samples, stride=2), :], wide[pl.ds(1, samples, stride=2), :]], axis=1
+            ).astype(jnp.bfloat16)
+            own, edge = foot_ref[slot, 0], foot_ref[slot, 1]
+            whole = jnp.dot(own_ref[jnp.minimum(own, blocks - 1)], data, preferred_element_type=jnp.float32)
+            rim = jnp.dot(edge_ref[jnp.minimum(edge, blocks - 1)], data, preferred_element_type=jnp.float32)
+            part[step, :cells] += jnp.where(own < blocks, whole, 0.0)
+            part[step, cells:] += jnp.where(edge < blocks, rim, 0.0)
+
+        if step < groups - 1:
+            for chunk in range(chunks):
+                reduce_copy(step + 1, chunk).start()
+
+    def owner_copy(step, chunk):
+        to = lax.rem(tile + step, tiles)
+        return pltpu.make_async_remote_copy(
+            src_ref=snd.at[chunk, to],
+            dst_ref=rcv.at[chunk, tile],
+            send_sem=tr_send.at[chunk, step],
+            recv_sem=tr_recv.at[chunk, step],
+            device_id=(me, to),
+            device_id_type=MESH,
+        )
+
+    for chunk in range(chunks):
+        span = pl.ds(chunk * piece, piece)
+        total = part[groups - 1, span]
+        for step in range(1, groups):
+            reduce_copy(step, chunk).wait_recv()
+            total = total + arrived[step - 1, span]
+        for p in range(2):
+            turned = total[:, p * width:(p + 1) * width].T
+            for to in range(tiles):
+                snd[chunk, to, p] = turned[to * per:(to + 1) * per]
+        for step in range(1, tiles):
+            owner_copy(step, chunk).start()
+    for chunk in range(chunks):
+        out_ref[chunk, tile] = snd[chunk, tile]
+    for chunk in range(chunks):
+        for step in range(1, tiles):
+            copy = owner_copy(step, chunk)
+            copy.wait_send()
+            copy.wait_recv()
+            origin = lax.rem(tile + tiles - step, tiles)
+            out_ref[chunk, origin] = rcv[chunk, origin]
+    for step in range(1, groups):
+        for chunk in range(chunks):
+            reduce_copy(step, chunk).wait_send()
+
+
+def exchange(data, foot, own_blocks, edge_blocks):
+    groups, tiles = lax.axis_size("aperture"), lax.axis_size("tile")
+    slots, samples, _, lines = data.shape
+    cells, extra = own_blocks.shape[1], edge_blocks.shape[1]
+    rows, width, piece = cells + extra, lines // groups, extra
+    chunks, per = rows // piece, lines // (groups * tiles)
+    out = (chunks, tiles, 2, per, piece)
+    vmem = pl.BlockSpec(memory_space=pltpu.VMEM)
+    hbm = pl.BlockSpec(memory_space=pl.ANY)
+    return pl.pallas_call(
+        functools.partial(exchange_kernel, groups, tiles),
+        out_shape=jax.ShapeDtypeStruct(out, jnp.float32),
+        in_specs=[hbm, pl.BlockSpec(memory_space=pltpu.SMEM), hbm, hbm],
+        out_specs=vmem,
+        scratch_shapes=[
+            pltpu.VMEM((groups, slots, 2 * samples, width), jnp.bfloat16),
+            pltpu.VMEM(own_blocks.shape, jnp.bfloat16),
+            pltpu.VMEM(edge_blocks.shape, jnp.bfloat16),
+            pltpu.VMEM((2 * samples, width), jnp.float32),
+            pltpu.VMEM((groups, rows, 2 * width), jnp.float32),
+            pltpu.VMEM((groups - 1, rows, 2 * width), jnp.float32),
+            pltpu.VMEM(out, jnp.float32),
+            pltpu.VMEM(out, jnp.float32),
+            pltpu.SemaphoreType.DMA((groups,)),
+            pltpu.SemaphoreType.DMA((2,)),
+            pltpu.SemaphoreType.DMA((groups - 1, chunks)),
+            pltpu.SemaphoreType.DMA((groups - 1, chunks)),
+            pltpu.SemaphoreType.DMA((chunks, tiles)),
+            pltpu.SemaphoreType.DMA((chunks, tiles)),
+        ],
+        compiler_params=pltpu.CompilerParams(
+            collective_id=0, has_side_effects=True, vmem_limit_bytes=48 * 1024 * 1024
+        ),
+    )(data, foot, own_blocks, edge_blocks)
+
+
+def split(value):
+    high = value.astype(jnp.bfloat16)
+    return high, (value - high.astype(jnp.float32)).astype(jnp.bfloat16)
+
+
+def image_kernel(
+    tiles, grid_ref, edges_ref, twist_ref, inner_high, inner_low, place_ref, out_ref
+):
+    per = edges_ref.shape[0]
+    chunks, piece = grid_ref.shape[0], grid_ref.shape[4]
+    inner = (chunks - 1) * piece
+    real, imag = [], []
+    for t in range(tiles):
+        for p, into in ((0, real), (1, imag)):
+            first = grid_ref[0, t, p]
+            if t > 0:
+                first = first + grid_ref[chunks - 1, t - 1, p]
+            into.append(jnp.concatenate([first] + [grid_ref[c, t, p] for c in range(1, chunks - 1)], axis=1))
+    h_real, h_imag = [], []
+    for q in range(tiles):
+        g_real, g_imag = real[0], imag[0]
+        for t in range(1, tiles):
+            angle = 2.0 * math.pi * (t * q % tiles) / tiles
+            c, s = math.cos(angle), math.sin(angle)
+            for factor, re, im in ((c, real[t], imag[t]), (s, -imag[t], real[t])):
+                if abs(factor) < 1e-12:
+                    continue
+                if abs(abs(factor) - 1.0) < 1e-12:
+                    g_real = g_real + re if factor > 0 else g_real - re
+                    g_imag = g_imag + im if factor > 0 else g_imag - im
+                else:
+                    g_real = g_real + factor * re
+                    g_imag = g_imag + factor * im
+        c, s = twist_ref[0, q:q + 1, :], twist_ref[1, q:q + 1, :]
+        h_real.append(g_real * c - g_imag * s)
+        h_imag.append(g_real * s + g_imag * c)
+    stacked = jnp.concatenate(h_real + h_imag, axis=0)
+    high, low = split(stacked)
+    both = jnp.concatenate([high, low], axis=0)
+    dot = functools.partial(jnp.dot, preferred_element_type=jnp.float32)
+    count = tiles * per
+
+    def times(index):
+        wide = dot(both, inner_high[index])
+        return wide[:2 * count] + wide[2 * count:] + dot(high, inner_low[index])
+
+    by_cos, by_sin = times(0), times(1)
+    z_real = (by_cos[:count] - by_sin[count:]).reshape(tiles, per, inner)
+    z_imag = (by_sin[:count] + by_cos[count:]).reshape(tiles, per, inner)
+
+    lower = edges_ref[:, 0:1][None]
+    upper = edges_ref[:, 1:2][None]
+    shape = (tiles, per, inner)
+    cells = lax.broadcasted_iota(jnp.int32, shape, 2) * tiles + lax.broadcasted_iota(jnp.int32, shape, 0)
+    inside = (cells >= lower) & (cells < upper)
+    span = (upper - lower).astype(jnp.float32)
+    offset = (cells - lower).astype(jnp.float32)
+    xi = jnp.where(inside, -1.0 + (2.0 * offset + 1.0) / span, 0.0)
+    base = 1.0 - xi * xi
+    weight = jnp.where(inside, base * jnp.sqrt(base), 0.0)
+
+    def over_line(value):
+        return jnp.sum(jnp.sum(value, axis=0), axis=-1, keepdims=True)[None]
+
+    prev, curr = jnp.ones_like(xi), 4.0 * xi
+    re_fix, im_fix = jnp.zeros_like(xi), jnp.zeros_like(xi)
+    for order in range(GORDER):
+        poly = prev if order == 0 else curr
+        weighted = weight * poly
+        denom = over_line(weighted * poly)
+        re_fix = re_fix + (over_line(weighted * z_real) / denom) * poly
+        im_fix = im_fix + (over_line(weighted * z_imag) / denom) * poly
+        if order >= 1:
+            nxt = xi * curr * (2.0 * (order + 2) / (order + 1)) - prev * ((order + 3) / (order + 1))
+            prev, curr = curr, nxt
+    fixed = (jnp.where(inside, re_fix, z_real), jnp.where(inside, im_fix, z_imag))
+
+    lanes = 128
+    strips = inner // lanes
+    lines = []
+    for strip in range(strips):
+        for value in fixed:
+            lines.append(
+                jnp.concatenate([value[q, :, strip * lanes:(strip + 1) * lanes] for q in range(tiles)], axis=1)
+            )
+    high, low = split(jnp.concatenate(lines, axis=0))
+    placed = dot(jnp.concatenate([high, low], axis=0), place_ref[...])
+    placed = placed[:strips * 2 * per] + placed[strips * 2 * per:]
+    for strip in range(strips):
+        for p in range(2):
+            at = (strip * 2 + p) * per
+            out_ref[p, :, strip * lanes * tiles:(strip + 1) * lanes * tiles] = placed[at:at + per]
+
+
+def tables(tiles, inner):
+    width = tiles * inner
+    twist = 2.0 * np.pi * np.outer(np.arange(tiles), np.arange(inner)) / width
+    twist = np.stack([np.cos(twist), np.sin(twist)]) / math.sqrt(width)
+    angle = 2.0 * np.pi * (np.outer(np.arange(inner), np.arange(inner)) % inner) / inner
+    table = np.stack([np.cos(angle), np.sin(angle)]).astype(np.float32)
+    high = table.astype(ml_dtypes.bfloat16)
+    low = (table - high.astype(np.float32)).astype(ml_dtypes.bfloat16)
+    lanes = 128
+    place = np.zeros((tiles, lanes, lanes * tiles), np.float32)
+    for q in range(tiles):
+        place[q, np.arange(lanes), np.arange(lanes) * tiles + q] = 1.0
+    place = place.reshape(tiles * lanes, lanes * tiles).astype(ml_dtypes.bfloat16)
+    return twist.astype(np.float32), high, low, place
+
+
+def form_image(grid, edges):
+    chunks, tiles, _, per, piece = grid.shape
+    inner = (chunks - 1) * piece
+    twist, high, low, place = tables(tiles, inner)
+    vmem = pl.BlockSpec(memory_space=pltpu.VMEM)
+    return pl.pallas_call(
+        functools.partial(image_kernel, tiles),
+        out_shape=jax.ShapeDtypeStruct((2, per, tiles * inner), jnp.float32),
+        in_specs=[vmem] * 6,
+        out_specs=vmem,
+        compiler_params=pltpu.CompilerParams(vmem_limit_bytes=40 * 1024 * 1024),
+    )(grid, edges, twist, high, low, place)
 
 
 def gegen_fix(field, edges):
@@ -74,49 +352,20 @@
     return jnp.stack([z_real, z_imag]).reshape(2, lines, width) * scale
 
 
+def form_image_wide(grid, edges):
+    chunks, tiles, _, per, piece = grid.shape
+    inner = (chunks - 1) * piece
+    first = grid[0] + jnp.pad(grid[-1, :-1], ((1, 0), (0, 0), (0, 0), (0, 0)))
+    blocks = jnp.concatenate([first[None], grid[1:-1]], axis=0)
+    field = blocks.transpose(2, 3, 1, 0, 4).reshape(2, per, tiles * inner)
+    return gegen_fix(spectral(field, tiles), edges)
+
+
 def on_device(sectors, footprint, own_blocks, edge_blocks, edges):
-    data = sectors[0]
-    foot = footprint[0]
-    slots = data.shape[0]
-    count_blocks = own_blocks.shape[0]
-    tile_rows = own_blocks.shape[1]
-    edge_rows = edge_blocks.shape[1]
-    lines = data.shape[3]
-    dims = (((0,), (1,)), ((), ()))
-
-    def apply_kernel(block, kernel):
-        return lax.dot_general(block, kernel, dims, preferred_element_type=jnp.float32)
-
-    def visit(slot, carry):
-        total, rim = carry
-        block = lax.dynamic_index_in_dim(data, slot, 0, keepdims=False)
-        own_index = foot[slot, 0]
-        edge_index = foot[slot, 1]
-        own_kernel = own_blocks[jnp.minimum(own_index, count_blocks - 1)]
-        edge_kernel = edge_blocks[jnp.minimum(edge_index, count_blocks - 1)]
-        total = total + jnp.where(own_index < count_blocks, apply_kernel(block, own_kernel), 0.0)
-        rim = rim + jnp.where(edge_index < count_blocks, apply_kernel(block, edge_kernel), 0.0)
-        return (total, rim)
-
-    start = (
-        jnp.zeros((2, lines, tile_rows), jnp.float32),
-        jnp.zeros((2, lines, edge_rows), jnp.float32),
-    )
-    total, rim = lax.fori_loop(0, slots, visit, start)
-    incoming = from_behind(rim, "tile", 1)
-    total = jnp.concatenate([total[:, :, :edge_rows] + incoming, total[:, :, edge_rows:]], axis=2)
-    groups = lax.axis_size("aperture")
-    tiles = lax.axis_size("tile")
-    per_device = lines // (groups * tiles)
-    stacked = total.reshape(2, groups, tiles * per_device, tile_rows)
-    summed = lax.psum_scatter(stacked, "aperture", scatter_dimension=1, tiled=True).reshape(
-        2, tiles, per_device, tile_rows
-    )
-    gathered = lax.all_to_all(summed, "tile", split_axis=1, concat_axis=3, tiled=True)
-    count = gathered.shape[2]
-    field = spectral(gathered.reshape(2, count, -1), tiles).reshape(2, 1, count, -1)
-    field = field.reshape(2, per_device, -1)
-    return gegen_fix(field, edges)
+    grid = exchange(sectors[0], footprint[0], own_blocks, edge_blocks)
+    if grid.shape[1] <= 8 and grid.shape[3] % 8 == 0:
+        return form_image(grid, edges)
+    return form_image_wide(grid, edges)
 
 
 def solution(mesh):

time: 273 us -> 55.4 us (0.20)
  waiting for transfers between devices: 92 us -> 0 us
  matrix products: 73.7 us -> 0 us
  Pallas kernels: 0 us -> 50.6 us
  local copies, waits for them, and re-layouts: 45.8 us -> 4.56 us
  loops' own time: 31.4 us -> 0 us
  between operations: 13.6 us -> 0.05 us
  other arithmetic: 7.52 us -> 0 us
  starting transfers between devices: 7 us -> 0 us
    unnamed x2 -> x0, waiting for transfers between devices: 75.5 us -> none
    dot_general x32 -> x0, matrix products: 73.7 us -> none  [the longest x24 50.2 us: apply_kernel(): lax.dot_general(block, kernel, dims, preferred_element_type=jnp.float32)]
    pallas_call x0 -> x2, Pallas kernels: none -> 50.6 us  [the longest x1 46.7 us: exchange(): pl.pallas_call(functools.partial(exchange_kernel, groups, tiles), out_sha...]
    another operation x1 -> x0, loops' own time: 31.4 us -> none  [on_device(): total, rim = lax.fori_loop(0, slots, visit, start)]
    unnamed x19 -> x13, local copies, waits for them, and re-layouts: 33.9 us -> 3.79 us
    all_to_all x1 -> x0, waiting for transfers between devices: 15.1 us -> none  [on_device(): lax.all_to_all(summed, 'tile', split_axis=1, concat_axis=3, tiled=True)]
    dynamic_slice x12 -> x0, local copies, waits for them, and re-layouts: 7.86 us -> none  [visit(): edge_index = foot[slot, 1]]
    all_to_all x1 -> x0, starting transfers between devices: 4.61 us -> none  [on_device(): lax.all_to_all(summed, 'tile', split_axis=1, concat_axis=3, tiled=True)]
  transfers between devices with their start and end apart: 3 -> 0, of which waited for: 3 -> 0; matrix products, arithmetic and copies ran while one was open for 1% -> 0% of each run, Pallas kernels for 0% -> 0%
where the time goes in v1:
time: 55.4 us; the launch traced here: 55.2 us
  Pallas kernels  50.6 us (91%)
  local copies, waits for them, and re-layouts  4.56 us (8%)
    pallas_call x1, Pallas kernels, exchange(): pl.pallas_call(functools.partial(exchange_kernel, groups, tiles), out_sha...  46.7 us
    pallas_call x1, Pallas kernels, form_image(): pl.pallas_call(functools.partial(image_kernel, tiles), out_shape=jax.Shap...  3.88 us
    unnamed x13, local copies, waits for them, and re-layouts  3.79 us

profile of v1, /device:TPU:0, one launch (start us, length us, event | category | flops | bytes accessed | tf_op | source)
XLA Modules:
  0.0 55.2 jit_solution(17570353306104133201)
XLA Ops:
  0.0 0.8 %copy.10.foot_ref = s32[12,2]{1,0:T(8,128)S(1)} copy(s32[12,2]{0,1:T(2,128)} %bitcast.3) | data formatting | bytes 192 | tf_op jit(solution)/shard_map/squeeze | solution.py:365
  0.8 0.8 %copy.11.edges_ref = s32[16,2]{1,0:T(8,128)S(1)} copy(s32[16,2]{0,1:T(2,128)} %param.13) | data formatting | bytes 256 | tf_op args[4]
  1.5 0.0 copy-start
  1.5 1.9 %copy-done = bf16[6,512,512]{2,1,0:T(8,128)(2,1)S(1)} copy-done((bf16[6,512,512]{2,1,0:T(8,128)(2,1)S(1)}, bf16[6,512,512]{2,1,0:T(8,128)(2,1)}, u32[]{:S(2)}) %copy-start) | copy-done | bytes 3145752
  3.4 0.0 copy-start.4
  3.4 1.1 %copy-done.4 = bf16[6,128,512]{2,1,0:T(8,128)(2,1)S(1)} copy-done((bf16[6,128,512]{2,1,0:T(8,128)(2,1)S(1)}, bf16[6,128,512]{2,1,0:T(8,128)(2,1)}, u32[]{:S(2)}) %copy-start.4) | copy-done | bytes 786456
  4.5 0.0 copy-start.1
  4.5 0.0 copy-start.2
  4.6 0.0 copy-start.3
  4.6 0.0 copy-start.5
  4.6 46.7 %shard_map.91.grid_ref = f32[5,8,2,16,128]{4,3,2,1,0:T(8,128)S(1)} custom-call(bf16[12,512,2,512]{3,2,1,0:T(2,128)(2,1)} %bitcast.2, s32[12,2]{1,0:T(8,128)S(1)} %copy.10.foot_ref, bf16[6,512,512]{2,1,0:T(8,128)(2,1)S(1)} %copy-done, bf16[6,128,512]{2,1,0:T(8,128)(2,1)S(1)} %copy-done.4), custom_call_target="tpu_custom_call" | custom-call | tf_op jit(solution)/shard_map/pallas_call | solution.py:144
  51.2 0.0 copy-done.1
  51.3 0.0 copy-done.2
  51.3 0.0 copy-done.3
  51.3 0.0 copy-done.5
  51.3 3.9 %shard_map.92 = f32[2,16,4096]{2,1,0:T(8,128)} custom-call(f32[5,8,2,16,128]{4,3,2,1,0:T(8,128)S(1)} %shard_map.91.grid_ref, s32[16,2]{1,0:T(8,128)S(1)} %copy.11.edges_ref, f32[2,8,512]{2,1,0:T(8,128)S(1)} %copy-done.5, bf16[2,512,512]{2,1,0:T(8,128)(2,1)S(1)} %copy-done.3, bf16[2,512,512]{2,1,0:T(8,128)(2,1)S(1)} %copy-done.2, bf16[1024,1024]{1,0:T(8,128)(2,1)S(1)} %copy-done.1), custom_call_target="tpu_custom_call" | custom-call | tf_op jit(solution)/shard_map/pallas_call | solution.py:286
Async XLA Ops:
  1.5 1.9 %copy-start = (bf16[6,512,512]{2,1,0:T(8,128)(2,1)S(1)}, bf16[6,512,512]{2,1,0:T(8,128)(2,1)}, u32[]{:S(2)}) copy-start(bf16[6,512,512]{2,1,0:T(8,128)(2,1)} %own_hbm.1) | copy-start | bytes 9437188
  3.4 1.1 %copy-start.4 = (bf16[6,128,512]{2,1,0:T(8,128)(2,1)S(1)}, bf16[6,128,512]{2,1,0:T(8,128)(2,1)}, u32[]{:S(2)}) copy-start(bf16[6,128,512]{2,1,0:T(8,128)(2,1)} %edge_hbm.1) | copy-start | bytes 2359300
  4.5 46.7 %copy-start.1 = (bf16[1024,1024]{1,0:T(8,128)(2,1)S(1)}, bf16[1024,1024]{1,0:T(8,128)(2,1)}, u32[]{:S(2)}) copy-start(bf16[1024,1024]{1,0:T(8,128)(2,1)} %constant.11.clone.place_ref) | copy-start | bytes 6291460
  4.5 46.7 %copy-start.2 = (bf16[2,512,512]{2,1,0:T(8,128)(2,1)S(1)}, bf16[2,512,512]{2,1,0:T(8,128)(2,1)}, u32[]{:S(2)}) copy-start(bf16[2,512,512]{2,1,0:T(8,128)(2,1)} %constant.10.clone.inner_low) | copy-start | bytes 3145732
  4.6 46.7 %copy-start.3 = (bf16[2,512,512]{2,1,0:T(8,128)(2,1)S(1)}, bf16[2,512,512]{2,1,0:T(8,128)(2,1)}, u32[]{:S(2)}) copy-start(bf16[2,512,512]{2,1,0:T(8,128)(2,1)} %constant.9.clone.inner_high) | copy-start | bytes 3145732
  4.6 46.7 %copy-start.5 = (f32[2,8,512]{2,1,0:T(8,128)S(1)}, f32[2,8,512]{2,1,0:T(8,128)}, u32[]{:S(2)}) copy-start(f32[2,8,512]{2,1,0:T(8,128)} %constant.8.clone.twist_ref) | copy-start | bytes 98308

commit v2 on v1

--- a/solution.py
+++ b/solution.py
@@ -14,33 +14,29 @@
 MESH = pl.DeviceIdType.MESH
 
 
-def partner(me, step, groups):
+def partners(me, groups):
     if groups == 4:
-        return [3 - me, me + 1 - 2 * lax.rem(me, 2), lax.rem(me + 2, 4)][step - 1]
-    return lax.rem(me + step, groups)
-
-
-def source(me, step, groups):
-    if groups == 4:
-        return partner(me, step, groups)
-    return lax.rem(me + groups - step, groups)
+        return [3 - me, lax.rem(me + 2, 4), me + 1 - 2 * lax.rem(me, 2)]
+    return [lax.rem(me + step, groups) for step in range(1, groups)]
 
 
 def exchange_kernel(
     groups, tiles, sec_ref, foot_ref, own_hbm, edge_hbm, out_ref,
-    held, own_ref, edge_ref, wide, part, arrived, snd, rcv,
-    load_sem, kern_sem, rs_send, rs_recv, tr_send, tr_recv,
+    held, own_ref, edge_ref, wide, part, rims, rims_in, arrived, snd, rcv,
+    load_sem, kern_sem, rim_send, rim_recv, rs_send, rs_recv, tr_send, tr_recv,
 ):
     slots, samples = sec_ref.shape[0], sec_ref.shape[1]
-    blocks, cells = own_ref.shape[0], own_ref.shape[1]
+    blocks, piece = edge_ref.shape[0], edge_ref.shape[1]
     rows, width = part.shape[1], part.shape[2] // 2
     chunks = snd.shape[0]
-    piece = rows // chunks
     per = snd.shape[3]
+    square = groups == 4
     me = lax.axis_index("aperture")
     tile = lax.axis_index("tile")
     flat = sec_ref.reshape(slots, 2 * samples, sec_ref.shape[3])
-    order = [partner(me, step, groups) for step in range(1, groups)] + [me]
+    others = partners(me, groups)
+    order = others + [me]
+    last = groups - 1
 
     def load(step):
         lanes = pl.ds(pl.multiple_of(order[step] * width, width), width)
@@ -56,28 +52,56 @@
         load(step).start()
 
     barrier = pltpu.get_barrier_semaphore()
-    for step in range(1, groups):
-        pl.semaphore_signal(barrier, inc=1, device_id=(partner(me, step, groups), tile), device_id_type=MESH)
+    greeted = others[1:] if square else others
+    for other in greeted:
+        pl.semaphore_signal(barrier, inc=1, device_id=(other, tile), device_id_type=MESH)
     for step in range(1, tiles):
         pl.semaphore_signal(barrier, inc=1, device_id=(me, lax.rem(tile + step, tiles)), device_id_type=MESH)
-    pl.semaphore_wait(barrier, groups + tiles - 2)
+    pl.semaphore_wait(barrier, len(greeted) + tiles - 1)
     for copy in kernels:
         copy.wait()
 
-    def reduce_copy(step, chunk):
-        span = pl.ds(chunk * piece, piece)
+    def span(chunk):
+        return pl.ds(chunk * piece, piece)
+
+    def rim_copy(step):
         return pltpu.make_async_remote_copy(
-            src_ref=part.at[step - 1, span],
-            dst_ref=arrived.at[step - 1, span],
-            send_sem=rs_send.at[step - 1, chunk],
-            recv_sem=rs_recv.at[step - 1, chunk],
-            device_id=(partner(me, step, groups), tile),
+            src_ref=rims.at[step],
+            dst_ref=rims_in.at[step],
+            send_sem=rim_send.at[step],
+            recv_sem=rim_recv.at[step],
+            device_id=(me, lax.rem(tile + 1, tiles)),
             device_id_type=MESH,
         )
+
+    def add_rim(step):
+        @pl.when(tile > 0)
+        def _():
+            rim_copy(step).wait_recv()
+            part[step, :piece] += rims_in[step]
+
+    def reduce_copy(step, chunk):
+        to = others[step]
+        if square and step == 0:
+            to = others[2 if chunk % 2 else 1]
+        return pltpu.make_async_remote_copy(
+            src_ref=part.at[step, span(chunk)],
+            dst_ref=arrived.at[step, span(chunk)],
+            send_sem=rs_send.at[step, chunk],
+            recv_sem=rs_recv.at[step, chunk],
+            device_id=(to, tile),
+            device_id_type=MESH,
+        )
+
+    def relay(step, chunk):
+        reduce_copy(0, chunk).wait_recv()
+        part[step, span(chunk)] += arrived[0, span(chunk)]
+        reduce_copy(step, chunk).start()
 
     for step in range(groups):
         load(step).wait()
         part[step] = jnp.zeros((rows, 2 * width), jnp.float32)
+        rims[step] = jnp.zeros((piece, 2 * width), jnp.float32)
 
         @pl.loop(0, slots)
         def _(slot):
@@ -88,12 +112,40 @@
             own, edge = foot_ref[slot, 0], foot_ref[slot, 1]
             whole = jnp.dot(own_ref[jnp.minimum(own, blocks - 1)], data, preferred_element_type=jnp.float32)
             rim = jnp.dot(edge_ref[jnp.minimum(edge, blocks - 1)], data, preferred_element_type=jnp.float32)
-            part[step, :cells] += jnp.where(own < blocks, whole, 0.0)
-            part[step, cells:] += jnp.where(edge < blocks, rim, 0.0)
-
-        if step < groups - 1:
-            for chunk in range(chunks):
-                reduce_copy(step + 1, chunk).start()
+            part[step] += jnp.where(own < blocks, whole, 0.0)
+            rims[step] += jnp.where(edge < blocks, rim, 0.0)
+
+        @pl.when(tile < tiles - 1)
+        def _():
+            rim_copy(step).start()
+
+        if not square:
+            if step > 0:
+                add_rim(step - 1)
+                reduce_copy(step - 1, 0).start()
+            if step < last:
+                for chunk in range(1, chunks):
+                    reduce_copy(step, chunk).start()
+        elif step == 0:
+            for chunk in range(1, chunks):
+                reduce_copy(0, chunk).start()
+        elif step == 1:
+            add_rim(0)
+            reduce_copy(0, 0).start()
+            for chunk in range(2, chunks, 2):
+                reduce_copy(1, chunk).start()
+        elif step == 2:
+            for chunk in range(1, chunks, 2):
+                reduce_copy(2, chunk).start()
+            for chunk in range(1, chunks, 2):
+                relay(1, chunk)
+            add_rim(1)
+            reduce_copy(1, 0).start()
+        else:
+            for chunk in range(2, chunks, 2):
+                relay(2, chunk)
+            add_rim(2)
+            relay(2, 0)
 
     def owner_copy(step, chunk):
         to = lax.rem(tile + step, tiles)
@@ -106,12 +158,14 @@
             device_id_type=MESH,
         )
 
-    for chunk in range(chunks):
-        span = pl.ds(chunk * piece, piece)
-        total = part[groups - 1, span]
-        for step in range(1, groups):
+    turn = list(range(1, chunks, 2)) + list(range(2, chunks, 2)) + [0]
+    for chunk in turn:
+        if chunk == 0:
+            add_rim(last)
+        total = part[last, span(chunk)]
+        for step in range(1 if square else 0, last):
             reduce_copy(step, chunk).wait_recv()
-            total = total + arrived[step - 1, span]
+            total = total + arrived[step, span(chunk)]
         for p in range(2):
             turned = total[:, p * width:(p + 1) * width].T
             for to in range(tiles):
@@ -120,23 +174,28 @@
             owner_copy(step, chunk).start()
     for chunk in range(chunks):
         out_ref[chunk, tile] = snd[chunk, tile]
-    for chunk in range(chunks):
+    for chunk in turn:
         for step in range(1, tiles):
             copy = owner_copy(step, chunk)
             copy.wait_send()
             copy.wait_recv()
             origin = lax.rem(tile + tiles - step, tiles)
             out_ref[chunk, origin] = rcv[chunk, origin]
-    for step in range(1, groups):
+    for step in range(last):
         for chunk in range(chunks):
             reduce_copy(step, chunk).wait_send()
+
+    @pl.when(tile < tiles - 1)
+    def _():
+        for step in range(groups):
+            rim_copy(step).wait_send()
 
 
 def exchange(data, foot, own_blocks, edge_blocks):
     groups, tiles = lax.axis_size("aperture"), lax.axis_size("tile")
     slots, samples, _, lines = data.shape
-    cells, extra = own_blocks.shape[1], edge_blocks.shape[1]
-    rows, width, piece = cells + extra, lines // groups, extra
+    rows, piece = own_blocks.shape[1], edge_blocks.shape[1]
+    width = lines // groups
     chunks, per = rows // piece, lines // (groups * tiles)
     out = (chunks, tiles, 2, per, piece)
     vmem = pl.BlockSpec(memory_space=pltpu.VMEM)
@@ -152,11 +211,15 @@
             pltpu.VMEM(edge_blocks.shape, jnp.bfloat16),
             pltpu.VMEM((2 * samples, width), jnp.float32),
             pltpu.VMEM((groups, rows, 2 * width), jnp.float32),
+            pltpu.VMEM((groups, piece, 2 * width), jnp.float32),
+            pltpu.VMEM((groups, piece, 2 * width), jnp.float32),
             pltpu.VMEM((groups - 1, rows, 2 * width), jnp.float32),
             pltpu.VMEM(out, jnp.float32),
             pltpu.VMEM(out, jnp.float32),
             pltpu.SemaphoreType.DMA((groups,)),
             pltpu.SemaphoreType.DMA((2,)),
+            pltpu.SemaphoreType.DMA((groups,)),
+            pltpu.SemaphoreType.DMA((groups,)),
             pltpu.SemaphoreType.DMA((groups - 1, chunks)),
             pltpu.SemaphoreType.DMA((groups - 1, chunks)),
             pltpu.SemaphoreType.DMA((chunks, tiles)),
@@ -178,14 +241,11 @@
 ):
     per = edges_ref.shape[0]
     chunks, piece = grid_ref.shape[0], grid_ref.shape[4]
-    inner = (chunks - 1) * piece
+    inner = chunks * piece
     real, imag = [], []
     for t in range(tiles):
         for p, into in ((0, real), (1, imag)):
-            first = grid_ref[0, t, p]
-            if t > 0:
-                first = first + grid_ref[chunks - 1, t - 1, p]
-            into.append(jnp.concatenate([first] + [grid_ref[c, t, p] for c in range(1, chunks - 1)], axis=1))
+            into.append(jnp.concatenate([grid_ref[c, t, p] for c in range(chunks)], axis=1))
     h_real, h_imag = [], []
     for q in range(tiles):
         g_real, g_imag = real[0], imag[0]
@@ -280,7 +340,7 @@
 
 def form_image(grid, edges):
     chunks, tiles, _, per, piece = grid.shape
-    inner = (chunks - 1) * piece
+    inner = chunks * piece
     twist, high, low, place = tables(tiles, inner)
     vmem = pl.BlockSpec(memory_space=pltpu.VMEM)
     return pl.pallas_call(
@@ -354,10 +414,8 @@
 
 def form_image_wide(grid, edges):
     chunks, tiles, _, per, piece = grid.shape
-    inner = (chunks - 1) * piece
-    first = grid[0] + jnp.pad(grid[-1, :-1], ((1, 0), (0, 0), (0, 0), (0, 0)))
-    blocks = jnp.concatenate([first[None], grid[1:-1]], axis=0)
-    field = blocks.transpose(2, 3, 1, 0, 4).reshape(2, per, tiles * inner)
+    inner = chunks * piece
+    field = grid.transpose(2, 3, 1, 0, 4).reshape(2, per, tiles * inner)
     return gegen_fix(spectral(field, tiles), edges)
 
 

time: 55.4 us -> 47.7 us (0.86)
  Pallas kernels: 50.6 us -> 42.9 us
    pallas_call x1, Pallas kernels: 46.7 us -> 39 us  [exchange(): pl.pallas_call(functools.partial(exchange_kernel, groups, tiles), out_sha...]
where the time goes in v2:
time: 47.7 us; the launch traced here: 47.5 us
  Pallas kernels  42.9 us (90%)
  local copies, waits for them, and re-layouts  4.56 us (10%)
    pallas_call x1, Pallas kernels, exchange(): pl.pallas_call(functools.partial(exchange_kernel, groups, tiles), out_sha...  39 us
    pallas_call x1, Pallas kernels, form_image(): pl.pallas_call(functools.partial(image_kernel, tiles), out_shape=jax.Shap...  3.88 us
    unnamed x13, local copies, waits for them, and re-layouts  3.79 us

profile of v2, /device:TPU:0, one launch (start us, length us, event | category | flops | bytes accessed | tf_op | source)
XLA Modules:
  0.0 47.5 jit_solution(14676490313290674145)
XLA Ops:
  0.0 0.8 %copy.10.foot_ref = s32[12,2]{1,0:T(8,128)S(1)} copy(s32[12,2]{0,1:T(2,128)} %bitcast.3) | data formatting | bytes 192 | tf_op jit(solution)/shard_map/squeeze | solution.py:423
  0.8 0.8 %copy.11.edges_ref = s32[16,2]{1,0:T(8,128)S(1)} copy(s32[16,2]{0,1:T(2,128)} %param.13) | data formatting | bytes 256 | tf_op args[4]
  1.5 0.0 copy-start
  1.5 1.9 %copy-done = bf16[6,512,512]{2,1,0:T(8,128)(2,1)S(1)} copy-done((bf16[6,512,512]{2,1,0:T(8,128)(2,1)S(1)}, bf16[6,512,512]{2,1,0:T(8,128)(2,1)}, u32[]{:S(2)}) %copy-start) | copy-done | bytes 3145752
  3.4 0.0 copy-start.4
  3.4 1.1 %copy-done.4 = bf16[6,128,512]{2,1,0:T(8,128)(2,1)S(1)} copy-done((bf16[6,128,512]{2,1,0:T(8,128)(2,1)S(1)}, bf16[6,128,512]{2,1,0:T(8,128)(2,1)}, u32[]{:S(2)}) %copy-start.4) | copy-done | bytes 786456
  4.5 0.0 copy-start.1
  4.5 0.0 copy-start.2
  4.6 0.0 copy-start.3
  4.6 0.0 copy-start.5
  4.6 39.0 %shard_map.91.grid_ref = f32[4,8,2,16,128]{4,3,2,1,0:T(8,128)S(1)} custom-call(bf16[12,512,2,512]{3,2,1,0:T(2,128)(2,1)} %bitcast.2, s32[12,2]{1,0:T(8,128)S(1)} %copy.10.foot_ref, bf16[6,512,512]{2,1,0:T(8,128)(2,1)S(1)} %copy-done, bf16[6,128,512]{2,1,0:T(8,128)(2,1)S(1)} %copy-done.4), custom_call_target="tpu_custom_call" | custom-call | tf_op jit(solution)/shard_map/pallas_call | solution.py:203
  43.6 0.0 copy-done.1
  43.6 0.0 copy-done.2
  43.6 0.0 copy-done.3
  43.6 0.0 copy-done.5
  43.6 3.9 %shard_map.92 = f32[2,16,4096]{2,1,0:T(8,128)} custom-call(f32[4,8,2,16,128]{4,3,2,1,0:T(8,128)S(1)} %shard_map.91.grid_ref, s32[16,2]{1,0:T(8,128)S(1)} %copy.11.edges_ref, f32[2,8,512]{2,1,0:T(8,128)S(1)} %copy-done.5, bf16[2,512,512]{2,1,0:T(8,128)(2,1)S(1)} %copy-done.3, bf16[2,512,512]{2,1,0:T(8,128)(2,1)S(1)} %copy-done.2, bf16[1024,1024]{1,0:T(8,128)(2,1)S(1)} %copy-done.1), custom_call_target="tpu_custom_call" | custom-call | tf_op jit(solution)/shard_map/pallas_call | solution.py:346
Async XLA Ops:
  1.5 1.9 %copy-start = (bf16[6,512,512]{2,1,0:T(8,128)(2,1)S(1)}, bf16[6,512,512]{2,1,0:T(8,128)(2,1)}, u32[]{:S(2)}) copy-start(bf16[6,512,512]{2,1,0:T(8,128)(2,1)} %own_hbm.1) | copy-start | bytes 9437188
  3.4 1.1 %copy-start.4 = (bf16[6,128,512]{2,1,0:T(8,128)(2,1)S(1)}, bf16[6,128,512]{2,1,0:T(8,128)(2,1)}, u32[]{:S(2)}) copy-start(bf16[6,128,512]{2,1,0:T(8,128)(2,1)} %edge_hbm.1) | copy-start | bytes 2359300
  4.5 39.0 %copy-start.1 = (bf16[1024,1024]{1,0:T(8,128)(2,1)S(1)}, bf16[1024,1024]{1,0:T(8,128)(2,1)}, u32[]{:S(2)}) copy-start(bf16[1024,1024]{1,0:T(8,128)(2,1)} %constant.11.clone.place_ref) | copy-start | bytes 6291460
  4.5 39.1 %copy-start.2 = (bf16[2,512,512]{2,1,0:T(8,128)(2,1)S(1)}, bf16[2,512,512]{2,1,0:T(8,128)(2,1)}, u32[]{:S(2)}) copy-start(bf16[2,512,512]{2,1,0:T(8,128)(2,1)} %constant.10.clone.inner_low) | copy-start | bytes 3145732
  4.6 39.1 %copy-start.3 = (bf16[2,512,512]{2,1,0:T(8,128)(2,1)S(1)}, bf16[2,512,512]{2,1,0:T(8,128)(2,1)}, u32[]{:S(2)}) copy-start(bf16[2,512,512]{2,1,0:T(8,128)(2,1)} %constant.9.clone.inner_high) | copy-start | bytes 3145732
  4.6 39.1 %copy-start.5 = (f32[2,8,512]{2,1,0:T(8,128)S(1)}, f32[2,8,512]{2,1,0:T(8,128)}, u32[]{:S(2)}) copy-start(f32[2,8,512]{2,1,0:T(8,128)} %constant.8.clone.twist_ref) | copy-start | bytes 98308

commit v3 on v2

--- a/solution.py
+++ b/solution.py
@@ -109,7 +109,7 @@
             data = jnp.concatenate(
                 [wide[pl.ds(0, samples, stride=2), :], wide[pl.ds(1, samples, stride=2), :]], axis=1
             ).astype(jnp.bfloat16)
-            own, edge = foot_ref[slot, 0], foot_ref[slot, 1]
+            own, edge = foot_ref[0, slot], foot_ref[1, slot]
             whole = jnp.dot(own_ref[jnp.minimum(own, blocks - 1)], data, preferred_element_type=jnp.float32)
             rim = jnp.dot(edge_ref[jnp.minimum(edge, blocks - 1)], data, preferred_element_type=jnp.float32)
             part[step] += jnp.where(own < blocks, whole, 0.0)
@@ -226,9 +226,9 @@
             pltpu.SemaphoreType.DMA((chunks, tiles)),
         ],
         compiler_params=pltpu.CompilerParams(
-            collective_id=0, has_side_effects=True, vmem_limit_bytes=48 * 1024 * 1024
+            collective_id=0, has_side_effects=True, vmem_limit_bytes=62 * 1024 * 1024
         ),
-    )(data, foot, own_blocks, edge_blocks)
+    )(data, foot.T, own_blocks, edge_blocks)
 
 
 def split(value):
@@ -237,9 +237,17 @@
 
 
 def image_kernel(
-    tiles, grid_ref, edges_ref, twist_ref, inner_high, inner_low, place_ref, out_ref
+    tiles, grid_ref, edges_ref, twist_ref, high_hbm, low_hbm, place_hbm, out_ref,
+    inner_high, inner_low, place_ref, sem,
 ):
-    per = edges_ref.shape[0]
+    per = edges_ref.shape[1]
+    loads = [
+        pltpu.make_async_copy(high_hbm, inner_high, sem.at[0]),
+        pltpu.make_async_copy(low_hbm, inner_low, sem.at[1]),
+        pltpu.make_async_copy(place_hbm, place_ref, sem.at[2]),
+    ]
+    for copy in loads:
+        copy.start()
     chunks, piece = grid_ref.shape[0], grid_ref.shape[4]
     inner = chunks * piece
     real, imag = [], []
@@ -274,12 +282,17 @@
         wide = dot(both, inner_high[index])
         return wide[:2 * count] + wide[2 * count:] + dot(high, inner_low[index])
 
+    loads[0].wait()
+    loads[1].wait()
     by_cos, by_sin = times(0), times(1)
     z_real = (by_cos[:count] - by_sin[count:]).reshape(tiles, per, inner)
     z_imag = (by_sin[:count] + by_cos[count:]).reshape(tiles, per, inner)
 
-    lower = edges_ref[:, 0:1][None]
-    upper = edges_ref[:, 1:2][None]
+    line = lax.broadcasted_iota(jnp.int32, (1, per, 1), 1)
+    lower = upper = jnp.zeros((1, per, 1), jnp.int32)
+    for at in range(per):
+        lower = jnp.where(line == at, edges_ref[0, at], lower)
+        upper = jnp.where(line == at, edges_ref[1, at], upper)
     shape = (tiles, per, inner)
     cells = lax.broadcasted_iota(jnp.int32, shape, 2) * tiles + lax.broadcasted_iota(jnp.int32, shape, 0)
     inside = (cells >= lower) & (cells < upper)
@@ -314,6 +327,7 @@
                 jnp.concatenate([value[q, :, strip * lanes:(strip + 1) * lanes] for q in range(tiles)], axis=1)
             )
     high, low = split(jnp.concatenate(lines, axis=0))
+    loads[2].wait()
     placed = dot(jnp.concatenate([high, low], axis=0), place_ref[...])
     placed = placed[:strips * 2 * per] + placed[strips * 2 * per:]
     for strip in range(strips):
@@ -343,13 +357,20 @@
     inner = chunks * piece
     twist, high, low, place = tables(tiles, inner)
     vmem = pl.BlockSpec(memory_space=pltpu.VMEM)
+    hbm = pl.BlockSpec(memory_space=pl.ANY)
     return pl.pallas_call(
         functools.partial(image_kernel, tiles),
         out_shape=jax.ShapeDtypeStruct((2, per, tiles * inner), jnp.float32),
-        in_specs=[vmem] * 6,
+        in_specs=[vmem, pl.BlockSpec(memory_space=pltpu.SMEM), vmem, hbm, hbm, hbm],
         out_specs=vmem,
-        compiler_params=pltpu.CompilerParams(vmem_limit_bytes=40 * 1024 * 1024),
-    )(grid, edges, twist, high, low, place)
+        scratch_shapes=[
+            pltpu.VMEM(high.shape, jnp.bfloat16),
+            pltpu.VMEM(low.shape, jnp.bfloat16),
+            pltpu.VMEM(place.shape, jnp.bfloat16),
+            pltpu.SemaphoreType.DMA((3,)),
+        ],
+        compiler_params=pltpu.CompilerParams(vmem_limit_bytes=62 * 1024 * 1024),
+    )(grid, edges.T, twist, high, low, place)
 
 
 def gegen_fix(field, edges):

time: 47.7 us -> 48.9 us (1.025)
  Pallas kernels: 42.9 us -> 48.7 us
  local copies, waits for them, and re-layouts: 4.56 us -> 0 us
    unnamed x13 -> x0, local copies, waits for them, and re-layouts: 3.79 us -> none
    pallas_call x1, Pallas kernels: 39 us -> 42.2 us  [exchange(): pl.pallas_call(functools.partial(exchange_kernel, groups, tiles), out_sha...]
    pallas_call x1, Pallas kernels: 3.88 us -> 6.55 us  [form_image(): pl.pallas_call(functools.partial(image_kernel, tiles), out_shape=jax.Shap...]
    squeeze x1 -> x0, local copies, waits for them, and re-layouts: 0.77 us -> none  [on_device(): grid = exchange(sectors[0], footprint[0], own_blocks, edge_blocks)]
where the time goes in v3:
time: 48.9 us; the launch traced here: 48.7 us
  Pallas kernels  48.7 us (100%)
    pallas_call x1, Pallas kernels, exchange(): pl.pallas_call(functools.partial(exchange_kernel, groups, tiles), out_sha...  42.2 us
    pallas_call x1, Pallas kernels, form_image(): pl.pallas_call(functools.partial(image_kernel, tiles), out_shape=jax.Shap...  6.55 us

profile of v3, /device:TPU:0, one launch (start us, length us, event | category | flops | bytes accessed | tf_op | source)
XLA Modules:
  0.0 48.7 jit_solution(6190263090649711116)
XLA Ops:
  0.0 42.2 %shard_map.91.grid_ref = f32[4,8,2,16,128]{4,3,2,1,0:T(8,128)} custom-call(bf16[12,512,2,512]{3,2,1,0:T(2,128)(2,1)} %bitcast.5, s32[2,12]{1,0:T(2,128)} %bitcast.6, bf16[6,512,512]{2,1,0:T(8,128)(2,1)} %own_hbm.1, bf16[6,128,512]{2,1,0:T(8,128)(2,1)} %edge_hbm.1), custom_call_target="tpu_custom_call" | custom-call | tf_op jit(solution)/shard_map/pallas_call | solution.py:203
  42.2 6.5 %shard_map.92 = f32[2,16,4096]{2,1,0:T(8,128)} custom-call(f32[4,8,2,16,128]{4,3,2,1,0:T(8,128)} %shard_map.91.grid_ref, s32[2,16]{1,0:T(2,128)} %bitcast.7, f32[2,8,512]{2,1,0:T(8,128)} %constant.8.clone.twist_ref, bf16[2,512,512]{2,1,0:T(8,128)(2,1)} %constant.9.clone.high_hbm, bf16[2,512,512]{2,1,0:T(8,128)(2,1)} %constant.10.clone.low_hbm, ...), custom_call_target="tpu_custom_call" | custom-call | tf_op jit(solution)/shard_map/pallas_call | solution.py:361

commit v4 on v2

--- a/solution.py
+++ b/solution.py
@@ -109,7 +109,7 @@
             data = jnp.concatenate(
                 [wide[pl.ds(0, samples, stride=2), :], wide[pl.ds(1, samples, stride=2), :]], axis=1
             ).astype(jnp.bfloat16)
-            own, edge = foot_ref[slot, 0], foot_ref[slot, 1]
+            own, edge = foot_ref[0, slot], foot_ref[1, slot]
             whole = jnp.dot(own_ref[jnp.minimum(own, blocks - 1)], data, preferred_element_type=jnp.float32)
             rim = jnp.dot(edge_ref[jnp.minimum(edge, blocks - 1)], data, preferred_element_type=jnp.float32)
             part[step] += jnp.where(own < blocks, whole, 0.0)
@@ -228,7 +228,7 @@
         compiler_params=pltpu.CompilerParams(
             collective_id=0, has_side_effects=True, vmem_limit_bytes=48 * 1024 * 1024
         ),
-    )(data, foot, own_blocks, edge_blocks)
+    )(data, foot.T, own_blocks, edge_blocks)
 
 
 def split(value):
@@ -239,7 +239,7 @@
 def image_kernel(
     tiles, grid_ref, edges_ref, twist_ref, inner_high, inner_low, place_ref, out_ref
 ):
-    per = edges_ref.shape[0]
+    per = edges_ref.shape[1]
     chunks, piece = grid_ref.shape[0], grid_ref.shape[4]
     inner = chunks * piece
     real, imag = [], []
@@ -278,8 +278,11 @@
     z_real = (by_cos[:count] - by_sin[count:]).reshape(tiles, per, inner)
     z_imag = (by_sin[:count] + by_cos[count:]).reshape(tiles, per, inner)
 
-    lower = edges_ref[:, 0:1][None]
-    upper = edges_ref[:, 1:2][None]
+    line = lax.broadcasted_iota(jnp.int32, (1, per, 1), 1)
+    lower = upper = jnp.zeros((1, per, 1), jnp.int32)
+    for at in range(per):
+        lower = jnp.where(line == at, edges_ref[0, at], lower)
+        upper = jnp.where(line == at, edges_ref[1, at], upper)
     shape = (tiles, per, inner)
     cells = lax.broadcasted_iota(jnp.int32, shape, 2) * tiles + lax.broadcasted_iota(jnp.int32, shape, 0)
     inside = (cells >= lower) & (cells < upper)
@@ -346,10 +349,10 @@
     return pl.pallas_call(
         functools.partial(image_kernel, tiles),
         out_shape=jax.ShapeDtypeStruct((2, per, tiles * inner), jnp.float32),
-        in_specs=[vmem] * 6,
+        in_specs=[vmem, pl.BlockSpec(memory_space=pltpu.SMEM)] + [vmem] * 4,
         out_specs=vmem,
         compiler_params=pltpu.CompilerParams(vmem_limit_bytes=40 * 1024 * 1024),
-    )(grid, edges, twist, high, low, place)
+    )(grid, edges.T, twist, high, low, place)
 
 
 def gegen_fix(field, edges):

time: 47.7 us -> 47.5 us (level)
  local copies, waits for them, and re-layouts: 4.56 us -> 3.72 us
  Pallas kernels: 42.9 us -> 43.5 us
    squeeze x1 -> x0, local copies, waits for them, and re-layouts: 0.77 us -> none  [on_device(): grid = exchange(sectors[0], footprint[0], own_blocks, edge_blocks)]
    pallas_call x1, Pallas kernels: 3.88 us -> 4.44 us  [form_image(): pl.pallas_call(functools.partial(image_kernel, tiles), out_shape=jax.Shap...]
    unnamed x13 -> x16, local copies, waits for them, and re-layouts: 3.79 us -> 3.72 us
where the time goes in v4:
time: 47.5 us; the launch traced here: 47.3 us
  Pallas kernels  43.5 us (92%)
  local copies, waits for them, and re-layouts  3.72 us (8%)
    pallas_call x1, Pallas kernels, exchange(): pl.pallas_call(functools.partial(exchange_kernel, groups, tiles), out_sha...  39 us
    pallas_call x1, Pallas kernels, form_image(): pl.pallas_call(functools.partial(image_kernel, tiles), out_shape=jax.Shap...  4.44 us
    unnamed x16, local copies, waits for them, and re-layouts  3.72 us

profile of v4, /device:TPU:0, one launch (start us, length us, event | category | flops | bytes accessed | tf_op | source)
XLA Modules:
  0.0 47.3 jit_solution(813833091406204658)
XLA Ops:
  0.0 0.0 copy-start
  0.0 1.9 %copy-done = bf16[6,512,512]{2,1,0:T(8,128)(2,1)S(1)} copy-done((bf16[6,512,512]{2,1,0:T(8,128)(2,1)S(1)}, bf16[6,512,512]{2,1,0:T(8,128)(2,1)}, u32[]{:S(2)}) %copy-start) | copy-done | bytes 3145752
  1.9 0.0 copy-start.4
  1.9 1.1 %copy-done.4 = bf16[6,128,512]{2,1,0:T(8,128)(2,1)S(1)} copy-done((bf16[6,128,512]{2,1,0:T(8,128)(2,1)S(1)}, bf16[6,128,512]{2,1,0:T(8,128)(2,1)}, u32[]{:S(2)}) %copy-start.4) | copy-done | bytes 786456
  3.0 0.0 copy-start.6
  3.0 0.7 %copy-done.6 = s32[1,12,2]{1,2,0:T(2,128)S(1)} copy-done((s32[1,12,2]{1,2,0:T(2,128)S(1)}, s32[1,12,2]{1,2,0:T(2,128)}, u32[]{:S(2)}) %copy-start.6) | copy-done | bytes 120
  3.7 0.0 copy-start.1
  3.7 0.0 copy-start.2
  3.7 0.0 copy-start.3
  3.7 0.0 copy-start.5
  3.7 0.0 copy-start.7
  3.7 39.0 %shard_map.91.grid_ref = f32[4,8,2,16,128]{4,3,2,1,0:T(8,128)S(1)} custom-call(bf16[12,512,2,512]{3,2,1,0:T(2,128)(2,1)} %bitcast.7, s32[2,12]{1,0:T(2,128)S(1)} %bitcast.5, bf16[6,512,512]{2,1,0:T(8,128)(2,1)S(1)} %copy-done, bf16[6,128,512]{2,1,0:T(8,128)(2,1)S(1)} %copy-done.4), custom_call_target="tpu_custom_call" | custom-call | tf_op jit(solution)/shard_map/pallas_call | solution.py:203
  42.8 0.0 copy-done.1
  42.8 0.0 copy-done.2
  42.8 0.0 copy-done.3
  42.8 0.0 copy-done.5
  42.8 0.0 copy-done.7
  42.8 4.4 %shard_map.92 = f32[2,16,4096]{2,1,0:T(8,128)} custom-call(f32[4,8,2,16,128]{4,3,2,1,0:T(8,128)S(1)} %shard_map.91.grid_ref, s32[2,16]{1,0:T(2,128)S(1)} %bitcast.6, f32[2,8,512]{2,1,0:T(8,128)S(1)} %copy-done.5, bf16[2,512,512]{2,1,0:T(8,128)(2,1)S(1)} %copy-done.3, bf16[2,512,512]{2,1,0:T(8,128)(2,1)S(1)} %copy-done.2, bf16[1024,1024]{1,0:T(8,128)(2,1)S(1)} %copy-done.1), custom_call_target="tpu_custom_call" | custom-call | tf_op jit(solution)/shard_map/pallas_call | solution.py:349
Async XLA Ops:
  0.0 1.9 %copy-start = (bf16[6,512,512]{2,1,0:T(8,128)(2,1)S(1)}, bf16[6,512,512]{2,1,0:T(8,128)(2,1)}, u32[]{:S(2)}) copy-start(bf16[6,512,512]{2,1,0:T(8,128)(2,1)} %own_hbm.1) | copy-start | bytes 9437188
  1.9 1.1 %copy-start.4 = (bf16[6,128,512]{2,1,0:T(8,128)(2,1)S(1)}, bf16[6,128,512]{2,1,0:T(8,128)(2,1)}, u32[]{:S(2)}) copy-start(bf16[6,128,512]{2,1,0:T(8,128)(2,1)} %edge_hbm.1) | copy-start | bytes 2359300
  3.0 0.7 %copy-start.6 = (s32[1,12,2]{1,2,0:T(2,128)S(1)}, s32[1,12,2]{1,2,0:T(2,128)}, u32[]{:S(2)}) copy-start(s32[1,12,2]{1,2,0:T(2,128)} %param.10) | copy-start | bytes 292
  3.7 39.1 %copy-start.1 = (bf16[1024,1024]{1,0:T(8,128)(2,1)S(1)}, bf16[1024,1024]{1,0:T(8,128)(2,1)}, u32[]{:S(2)}) copy-start(bf16[1024,1024]{1,0:T(8,128)(2,1)} %constant.11.clone.place_ref) | copy-start | bytes 6291460
  3.7 39.1 %copy-start.2 = (bf16[2,512,512]{2,1,0:T(8,128)(2,1)S(1)}, bf16[2,512,512]{2,1,0:T(8,128)(2,1)}, u32[]{:S(2)}) copy-start(bf16[2,512,512]{2,1,0:T(8,128)(2,1)} %constant.10.clone.inner_low) | copy-start | bytes 3145732
  3.7 39.1 %copy-start.3 = (bf16[2,512,512]{2,1,0:T(8,128)(2,1)S(1)}, bf16[2,512,512]{2,1,0:T(8,128)(2,1)}, u32[]{:S(2)}) copy-start(bf16[2,512,512]{2,1,0:T(8,128)(2,1)} %constant.9.clone.inner_high) | copy-start | bytes 3145732
  3.7 39.1 %copy-start.5 = (f32[2,8,512]{2,1,0:T(8,128)S(1)}, f32[2,8,512]{2,1,0:T(8,128)}, u32[]{:S(2)}) copy-start(f32[2,8,512]{2,1,0:T(8,128)} %constant.8.clone.twist_ref) | copy-start | bytes 98308
  3.7 39.1 %copy-start.7 = (s32[16,2]{0,1:T(2,128)S(1)}, s32[16,2]{0,1:T(2,128)}, u32[]{:S(2)}) copy-start(s32[16,2]{0,1:T(2,128)} %param.13) | copy-start | bytes 388
